TPU v7x, 32 devices: a whole 2x2x4 slice. The times are simulated.
32 devices in a mesh: groups: 2 (over y), tile: 4 (over z), cone: 2 (over x), rep: 2 (over core).
Axes of the slice: x: 2, y: 2, z: 4, core: 2. Of those that a mesh axis runs over, the one named last changes fastest.
Arguments:
- values: bfloat16 [1024, 6144], P(('groups', 'tile'), ('cone', 'rep')), parts along dimension 0, may hold values from -0.0546875 to 0.0546875
- pattern: int32 [8, 48], P(('groups', 'tile'), ('cone', 'rep')), parts along dimension 0, may hold values from 0 to 1, as said below
- cone_point: float32 [96, 128], P(('groups', 'cone', 'rep')), parts along dimension 0, may hold values from -1 to 2, as said below
- cone_scale: float32 [96], P(('groups', 'cone', 'rep')), parts along dimension 0, may hold values from 0.5 to 2
Outputs:
- schur: float32 [1024, 512], P(('groups', 'tile', 'cone', 'rep')), parts along dimension 0
There are 2 independent parts, one for each index of `groups`. A program takes and returns all parts, laid end to end along the dimension named above; each array names one. Nothing has to cross between parts.
Inputs may be any that keep to these rules, and one draw needn't show every extreme that they name: `pattern`: entries are 0 or 1. Among the 12 tiles of one row block in one column group (columns of 12 consecutive cones starting at a multiple of 12) at least 1 and at most 6 are 1; every row block has exactly 6 in some column group. `cone_point`: in every row the first entry is larger than the Euclidean length of the other entries by a margin, so det stays at 0.19 or more.
All inputs are finite; a program needn't handle non-finite values.
Results may differ from a plain program's by a relative error of at most 0.0018.
Values may be sent and summed in bfloat16 or wider, within the bound.
A program may use at most 64 MiB of HBM per device.

v0:
```python
import jax
import jax.numpy as jnp
from jax import lax
from jax.sharding import PartitionSpec as P


def arrow_scaled(tiles, cone_point, cone_scale):
    width = cone_point.shape[1]
    head = cone_point[:, 0]
    tail = cone_point[:, 1:]
    det = head * head - jnp.sum(tail * tail, axis=1)
    unit = cone_point / jnp.sqrt(det)[:, None]
    signs = jnp.where(jnp.arange(width) == 0, 1.0, -1.0).astype(jnp.float32)
    blocks = tiles.astype(jnp.float32)
    proj = jnp.einsum("rkc,kc->rk", blocks, unit, precision=lax.Precision.HIGHEST)
    factor = cone_scale[None, :, None]
    return (
        factor * (2.0 * proj[:, :, None] * unit[None, :, :] - blocks * signs[None, None, :])
    ).astype(jnp.bfloat16)


def per_device(values, pattern, cone_point, cone_scale):
    rows, cols = values.shape
    cones, width = cone_point.shape
    live = pattern[0].astype(jnp.bfloat16)
    masked_tiles = values.reshape(rows, cones, width) * live[None, :, None]
    scaled_tiles = arrow_scaled(masked_tiles, cone_point, cone_scale)
    scaled = scaled_tiles.reshape(rows, cols)
    block = lax.dot_general(
        scaled,
        lax.all_gather(scaled, "tile", axis=0, tiled=True),
        (((1,), (1,)), ((), ())),
        preferred_element_type=jnp.float32,
    )
    return lax.psum_scatter(block, ("cone", "rep"), scatter_dimension=0, tiled=True)


def solution(mesh):
    return jax.shard_map(
        per_device,
        mesh=mesh,
        in_specs=(
            P(("groups", "tile"), ("cone", "rep")),
            P(("groups", "tile"), ("cone", "rep")),
            P(("groups", "cone", "rep"), None),
            P(("groups", "cone", "rep")),
        ),
        out_specs=P(("groups", "tile", "cone", "rep"), None),
        check_vma=False,
    )
```

profile of v0, /device:TPU:0, one launch (start us, length us, event | category | flops | bytes accessed | tf_op | source)
XLA Modules:
  0.0 82.4 jit_solution(12743382015539982700)
XLA Ops:
  6.5 0.0 all-gather.2.cloned.1.call-start
  6.5 0.7 convert_bitcast_fusion
  7.2 0.9 %multiply_reduce_fusion = f32[12]{0:T(128)S(1)} fusion(f32[12,128]{1,0:T(8,128)} %param.6), kind=kLoop, calls=%fused_computation.9 | loop fusion | flops 3036 | bytes 6144 | tf_op jit(solution)/shard_map/reduce_sum | solution.py:11
  8.1 0.8 copy.11
  8.9 0.1 broadcast_bitcast_fusion.2
  8.9 0.8 fusion.9
  9.7 1.2 %copy.7 = bf16[128,1536]{0,1:T(8,128)(2,1)S(1)} copy(bf16[128,1536]{1,0:T(8,128)(2,1)} %param.4) | data formatting | bytes 786432 | tf_op args[0]
  10.9 0.5 fusion.3
  11.4 0.7 broadcast_bitcast_fusion
  12.2 1.6 %fusion.2 = bf16[128,1536]{0,1:T(8,128)(2,1)} fusion(f32[1536]{0:T(1024)S(1)} %get-tuple-element.7, bf16[128,1536]{0,1:T(8,128)(2,1)S(1)} %copy.7, f32[1536]{0:T(1024)S(1)} %get-tuple-element.6, f32[128,12]{0,1:T(8,128)S(1)} %fusion.6, f32[1536]{0:T(1024)S(1)} %get-tuple-element.8, bf16[1536]{0:T(1024)(128)(2,1)S(1)} %broadcast_bitcast_fusion.2), kind=kLoop, calls=%fused_computation.3 | loop fusion | flops 1376256 | bytes 814080 | tf_op jit(solution)/shard_map/convert_element_type | solution.py:19
  13.8 0.0 all-gather.2.cloned.1.call-update
  13.8 0.0 reduce-scatter.2.cloned.1.call-start
  13.9 40.5 %all-gather.2.cloned.1.call-done = bf16[512,1536]{0,1:T(8,128)(2,1)} async-done(((bf16[128,1536]{0,1:T(8,128)(2,1)}), bf16[512,1536]{0,1:T(8,128)(2,1)}) %all-gather.2.cloned.1.call-update) | async-done | bytes 1572880 | tf_op jit(solution)/shard_map/all_gather | solution.py:31
  54.4 2.7 %fusion.12 = f32[128,512]{1,0:T(8,128)} fusion(bf16[128,1536]{0,1:T(8,128)(2,1)} %fusion.2, bf16[512,1536]{0,1:T(8,128)(2,1)} %all-gather.2.cloned.1.call-done), kind=kOutput, calls=%fused_computation.22 | convolution fusion | flops 201326592 | bytes 2228224 | tf_op jit(solution)/shard_map/dot_general | solution.py:29
  57.1 0.0 reduce-scatter.2.cloned.1.call-update
  57.1 18.4 %reduce-scatter.2.cloned.1.call-done = f32[32,512]{1,0:T(8,128)} async-done(((f32[128,512]{1,0:T(8,128)}), f32[32,512]{1,0:T(8,128)}) %reduce-scatter.2.cloned.1.call-update) | async-done | bytes 65552 | tf_op jit(solution)/shard_map/reduce_scatter | solution.py:35
  (3 shorter events, 0.0 us)
Async XLA Ops:
  6.5 47.9 %all-gather.2.cloned.1.call-start = ((), (), s32[]{:S(2)}) async-start(), calls=%async_computation.1 | async-start | bytes 1966080 | tf_op jit(solution)/shard_map/all_gather | solution.py:31
  13.8 61.7 %reduce-scatter.2.cloned.1.call-start = ((), (), s32[]{:S(2)}) async-start(), calls=%async_computation.2 | async-start | bytes 327680 | tf_op jit(solution)/shard_map/reduce_scatter | solution.py:35
Sparse Core Ops, SparseCore 0:
  14.0 40.3 all-gather.1
  57.2 18.2 reduce-scatter.1
where the time goes:
time: 82.7 us; the launch traced here: 82.4 us
  waiting for transfers between devices  59 us (71%)
  between operations  13.4 us (16%)
  other arithmetic  3.97 us (5%)
  matrix products  3.15 us (4%)
  local copies, waits for them, and re-layouts  2.81 us (3%)
    all_gather x1, waiting for transfers between devices, per_device(): lax.all_gather(scaled, 'tile', axis=0, tiled=True)  40.5 us
    reduce_scatter x1, waiting for transfers between devices, per_device(): lax.psum_scatter(block, ('cone', 'rep'), scatter_dimension=0, tiled=True)  18.4 us
    dot_general x1, matrix products, per_device(): lax.dot_general(scaled, lax.all_gather(scaled, 'tile', axis=0, tiled=True...  2.67 us
    unnamed x2, local copies, waits for them, and re-layouts  2 us
  transfers between devices with their start and end apart: 2, of which 2 were waited for; matrix products, arithmetic and copies ran while one was open for 0% of the time, Pallas kernels for 0%

commit v1 on v0

v1 whole, which is shorter than its diff:
```python
import functools

import jax
import jax.numpy as jnp
from jax import lax
from jax.experimental import pallas as pl
from jax.experimental.pallas import tpu as pltpu
from jax.sharding import PartitionSpec as P

MESH = pl.DeviceIdType.MESH
SLOTS = 6


def kernel(n_tile, n_cone, n_rep, pattern_ref, scale_ref, values_ref, point_ref, out_ref,
           unit_ref, held, ids, part, landed, send_sem, recv_sem, part_send, part_recv):
    rows = values_ref.shape[0]
    cones, width = point_ref.shape
    n_sum = n_cone * n_rep
    strip = rows // n_sum
    me = lax.axis_index("tile")
    here = lax.axis_index("cone") * n_rep + lax.axis_index("rep")
    has_left, has_right = me > 0, me < n_tile - 1

    def peer(d):
        other = lax.rem(here + d, n_sum)
        return other, {"cone": other // n_rep, "rep": lax.rem(other, n_rep)}

    barrier = pltpu.get_barrier_semaphore()

    @pl.when(has_left)
    def _():
        pl.semaphore_signal(barrier, inc=1, device_id={"tile": me - 1}, device_id_type=MESH)

    @pl.when(has_right)
    def _():
        pl.semaphore_signal(barrier, inc=1, device_id={"tile": me + 1}, device_id_type=MESH)

    for d in range(1, n_sum):
        pl.semaphore_signal(barrier, inc=1, device_id=peer(d)[1], device_id_type=MESH)

    chosen = [[] for _ in range(SLOTS)]
    count = jnp.int32(0)
    for k in range(cones):
        live = pattern_ref[0, k]
        for s in range(SLOTS):
            chosen[s].append(live * (count == s).astype(jnp.int32) if k >= s else None)
        count = count + live
    for s in range(SLOTS):
        name = sum(chosen[s][k] * (k + 1) for k in range(s, cones))
        ids[me, s : s + 1, :] = jnp.full((1, width), name, jnp.int32)

    lane = lax.broadcasted_iota(jnp.int32, (1, width), 1)
    signs = jnp.where(lane == 0, 1.0, -1.0).astype(jnp.float32)
    point = point_ref[...]
    det = jnp.sum(point * point * signs, axis=1, keepdims=True)
    unit_ref[...] = point / jnp.sqrt(det)

    def block_copy(src, piece, right):
        ref = ids.at[src] if piece == SLOTS else held.at[src, piece]
        return pltpu.make_async_remote_copy(
            src_ref=ref,
            dst_ref=ref,
            send_sem=send_sem.at[0 if right else 1, src, piece],
            recv_sem=recv_sem.at[src, piece],
            device_id={"tile": me + 1 if right else me - 1},
            device_id_type=MESH,
        )

    def send_own(piece):
        @pl.when(has_right)
        def _():
            block_copy(me, piece, True).start()

        @pl.when(has_left)
        def _():
            block_copy(me, piece, False).start()

    pl.semaphore_wait(
        barrier, has_left.astype(jnp.int32) + has_right.astype(jnp.int32) + (n_sum - 1)
    )
    send_own(SLOTS)
    for s in range(SLOTS):
        factor, unit, packed = 0.0, 0.0, None
        for k in range(s, cones):
            weight = chosen[s][k].astype(jnp.float32)
            factor = factor + weight * scale_ref[k]
            unit = unit + weight * unit_ref[k : k + 1, :]
            mask = jnp.full((1, width), weight, jnp.float32).astype(jnp.bfloat16)
            term = values_ref[:, k * width : (k + 1) * width] * mask
            packed = term if packed is None else packed + term
        tile = packed.astype(jnp.float32)
        proj = jnp.sum(tile * unit, axis=1, keepdims=True)
        held[me, s] = (factor * (2.0 * proj * unit - tile * signs)).astype(jnp.bfloat16)
        send_own(s)

    def part_copy(src, d):
        other, device = peer(d)
        return pltpu.make_async_remote_copy(
            src_ref=part.at[src, other],
            dst_ref=landed.at[src, d - 1],
            send_sem=part_send.at[src, d - 1],
            recv_sem=part_recv.at[src, d - 1],
            device_id=device,
            device_id_type=MESH,
        )

    def product(src, own):
        mine = [held[me, s] for s in range(SLOTS)]
        if own:
            left = mine
        else:
            left = []
            for b in range(SLOTS):
                total = None
                for a in range(SLOTS):
                    same = (ids[me, a : a + 1, :] == ids[src, b : b + 1, :]).astype(jnp.float32)
                    term = mine[a] * same.astype(jnp.bfloat16)
                    total = term if total is None else total + term
                left.append(total)
        block = lax.dot_general(
            jnp.concatenate(left, axis=1),
            jnp.concatenate([held[src, s] for s in range(SLOTS)], axis=1),
            (((1,), (1,)), ((), ())),
            preferred_element_type=jnp.float32,
        )
        part[src] = block.reshape(n_sum, strip, width)
        for d in range(1, n_sum):
            part_copy(src, d).start()

    product(me, True)

    def step(s, carry):
        from_left, from_right = me - s, me + s
        for piece in (SLOTS, *range(SLOTS)):
            @pl.when(from_left >= 0)
            def _():
                block_copy(from_left, piece, True).wait_recv()

                @pl.when(has_right)
                def _():
                    block_copy(from_left, piece, True).start()

            @pl.when(from_right < n_tile)
            def _():
                block_copy(from_right, piece, False).wait_recv()

                @pl.when(has_left)
                def _():
                    block_copy(from_right, piece, False).start()

        @pl.when(from_left >= 0)
        def _():
            product(from_left, False)

        @pl.when(from_right < n_tile)
        def _():
            product(from_right, False)

        return carry

    lax.fori_loop(1, n_tile, step, 0)

    for src in range(n_tile):
        total = part[src, here]
        for d in range(1, n_sum):
            part_copy(src, d).wait_recv()
            total = total + landed[src, d - 1]
        out_ref[:, src * rows : (src + 1) * rows] = total

    def drain(src, carry):
        for d in range(1, n_sum):
            part_copy(src, d).wait_send()

        @pl.when(jnp.logical_and(has_right, src <= me))
        def _():
            for piece in range(SLOTS + 1):
                block_copy(src, piece, True).wait_send()

        @pl.when(jnp.logical_and(has_left, src >= me))
        def _():
            for piece in range(SLOTS + 1):
                block_copy(src, piece, False).wait_send()

        return carry

    lax.fori_loop(0, n_tile, drain, 0)


def solution(mesh):
    n_tile, n_cone, n_rep = mesh.shape["tile"], mesh.shape["cone"], mesh.shape["rep"]
    n_sum = n_cone * n_rep

    def per_device(values, pattern, cone_point, cone_scale):
        rows, cols = values.shape
        cones, width = cone_point.shape
        strip = rows // n_sum
        vmem = pl.BlockSpec(memory_space=pltpu.VMEM)
        smem = pl.BlockSpec(memory_space=pltpu.SMEM)
        return pl.pallas_call(
            functools.partial(kernel, n_tile, n_cone, n_rep),
            out_shape=jax.ShapeDtypeStruct((strip, n_tile * rows), jnp.float32),
            in_specs=[smem, smem, vmem, vmem],
            out_specs=vmem,
            scratch_shapes=[
                pltpu.VMEM((cones, width), jnp.float32),
                pltpu.VMEM((n_tile, SLOTS, rows, width), jnp.bfloat16),
                pltpu.VMEM((n_tile, 8, width), jnp.int32),
                pltpu.VMEM((n_tile, n_sum, strip, rows), jnp.float32),
                pltpu.VMEM((n_tile, n_sum - 1, strip, rows), jnp.float32),
                pltpu.SemaphoreType.DMA((2, n_tile, SLOTS + 1)),
                pltpu.SemaphoreType.DMA((n_tile, SLOTS + 1)),
                pltpu.SemaphoreType.DMA((n_tile, n_sum - 1)),
                pltpu.SemaphoreType.DMA((n_tile, n_sum - 1)),
            ],
            compiler_params=pltpu.CompilerParams(
                collective_id=0, has_side_effects=True, vmem_limit_bytes=32 * 1024 * 1024
            ),
        )(pattern, cone_scale, values, cone_point)

    return jax.shard_map(
        per_device,
        mesh=mesh,
        in_specs=(
            P(("groups", "tile"), ("cone", "rep")),
            P(("groups", "tile"), ("cone", "rep")),
            P(("groups", "cone", "rep"), None),
            P(("groups", "cone", "rep")),
        ),
        out_specs=P(("groups", "tile", "cone", "rep"), None),
        check_vma=False,
    )
```

time: 82.7 us -> 27 us (0.33)
  waiting for transfers between devices: 59 us -> 0 us
  Pallas kernels: 0 us -> 23.2 us
  between operations: 13.4 us -> 0.01 us
  other arithmetic: 3.97 us -> 0 us
  matrix products: 3.15 us -> 0 us
    all_gather x1 -> x0, waiting for transfers between devices: 40.5 us -> none  [per_device(): lax.all_gather(scaled, 'tile', axis=0, tiled=True)]
    pallas_call x0 -> x1, Pallas kernels: none -> 23.2 us  [per_device(): pl.pallas_call(functools.partial(kernel, n_tile, n_cone, n_rep), out_shap...]
    reduce_scatter x1 -> x0, waiting for transfers between devices: 18.4 us -> none  [per_device(): lax.psum_scatter(block, ('cone', 'rep'), scatter_dimension=0, tiled=True)]
    dot_general x2 -> x0, matrix products: 3.15 us -> none  [the longest x1 2.67 us: per_device(): lax.dot_general(scaled, lax.all_gather(scaled, 'tile', axis=0, tiled=True...]
    convert_element_type x2 -> x0, other arithmetic: 2.3 us -> none  [the longest x1 1.64 us: arrow_scaled(): return (factor * (2.0 * proj[:, :, None] * unit[None, :, :] - blocks * si...]
    unnamed x2 -> x9, local copies, waits for them, and re-layouts: 2 us -> 3.63 us
    reduce_sum x1 -> x0, other arithmetic: 0.88 us -> none  [arrow_scaled(): det = head * head - jnp.sum(tail * tail, axis=1)]
  transfers between devices with their start and end apart: 2 -> 0, of which waited for: 2 -> 0; matrix products, arithmetic and copies ran while one was open for 0% -> 0% of each run, Pallas kernels for 0% -> 0%
where the time goes in v1:
time: 27 us; the launch traced here: 26.8 us
  Pallas kernels  23.2 us (86%)
  local copies, waits for them, and re-layouts  3.63 us (13%)
    pallas_call x1, Pallas kernels, per_device(): pl.pallas_call(functools.partial(kernel, n_tile, n_cone, n_rep), out_shap...  23.2 us
    unnamed x9, local copies, waits for them, and re-layouts  3.63 us

profile of v1, /device:TPU:0, one launch (start us, length us, event | category | flops | bytes accessed | tf_op | source)
XLA Modules:
  0.0 26.8 jit_solution(10183447118894802181)
XLA Ops:
  0.0 0.0 copy-start
  0.0 1.0 %copy-done = bf16[128,1536]{1,0:T(8,128)(2,1)S(1)} copy-done((bf16[128,1536]{1,0:T(8,128)(2,1)S(1)}, bf16[128,1536]{1,0:T(8,128)(2,1)}, u32[]{:S(2)}) %copy-start) | copy-done | bytes 393240
  1.0 0.0 copy-start.1
  1.0 0.7 %copy-done.1 = f32[12,128]{1,0:T(8,128)S(1)} copy-done((f32[12,128]{1,0:T(8,128)S(1)}, f32[12,128]{1,0:T(8,128)}, u32[]{:S(2)}) %copy-start.1) | copy-done | bytes 6168
  1.7 0.0 copy-start.2
  1.7 0.7 %copy-done.2 = s32[1,12]{1,0:T(1,128)S(1)} copy-done((s32[1,12]{1,0:T(1,128)S(1)}, s32[1,12]{1,0:T(1,128)}, u32[]{:S(2)}) %copy-start.2) | copy-done | bytes 72
  2.4 0.0 copy-start.3
  2.4 0.7 %copy-done.3 = f32[12]{0:T(128)S(1)} copy-done((f32[12]{0:T(128)S(1)}, f32[12]{0:T(128)}, u32[]{:S(2)}) %copy-start.3) | copy-done | bytes 72
  3.0 23.2 %shard_map.46 = f32[32,512]{1,0:T(8,128)S(1)} custom-call(s32[1,12]{1,0:T(1,128)S(1)} %copy-done.2, f32[12]{0:T(128)S(1)} %copy-done.3, bf16[128,1536]{1,0:T(8,128)(2,1)S(1)} %copy-done, f32[12,128]{1,0:T(8,128)S(1)} %copy-done.1), custom_call_target="tpu_custom_call" | custom-call | tf_op jit(solution)/shard_map/pallas_call | solution.py:199
  26.2 0.6 %copy.6 = f32[32,512]{1,0:T(8,128)} copy(f32[32,512]{1,0:T(8,128)S(1)} %shard_map.46) | data formatting | bytes 131072
Async XLA Ops:
  0.0 1.0 %copy-start = (bf16[128,1536]{1,0:T(8,128)(2,1)S(1)}, bf16[128,1536]{1,0:T(8,128)(2,1)}, u32[]{:S(2)}) copy-start(bf16[128,1536]{1,0:T(8,128)(2,1)} %values_ref.1) | copy-start | bytes 1179652
  1.0 0.7 %copy-start.1 = (f32[12,128]{1,0:T(8,128)S(1)}, f32[12,128]{1,0:T(8,128)}, u32[]{:S(2)}) copy-start(f32[12,128]{1,0:T(8,128)} %point_ref.1) | copy-start | bytes 18436
  1.7 0.7 %copy-start.2 = (s32[1,12]{1,0:T(1,128)S(1)}, s32[1,12]{1,0:T(1,128)}, u32[]{:S(2)}) copy-start(s32[1,12]{1,0:T(1,128)} %pattern_ref.1) | copy-start | bytes 148
  2.4 0.7 %copy-start.3 = (f32[12]{0:T(128)S(1)}, f32[12]{0:T(128)}, u32[]{:S(2)}) copy-start(f32[12]{0:T(128)} %scale_ref.1) | copy-start | bytes 148

commit v2 on v1

--- a/solution.py
+++ b/solution.py
@@ -11,8 +11,8 @@
 SLOTS = 6
 
 
-def kernel(n_tile, n_cone, n_rep, pattern_ref, scale_ref, values_ref, point_ref, out_ref,
-           unit_ref, held, ids, part, landed, send_sem, recv_sem, part_send, part_recv):
+def kernel(n_tile, n_cone, n_rep, pattern_hbm, scale_hbm, values_hbm, point_hbm, out_ref,
+           pattern_ref, scale_ref, values_ref, point_ref, load_sem, unit_ref, held, ids, part, landed, send_sem, recv_sem, part_send, part_recv):
     rows = values_ref.shape[0]
     cones, width = point_ref.shape
     n_sum = n_cone * n_rep
@@ -37,6 +37,21 @@
 
     for d in range(1, n_sum):
         pl.semaphore_signal(barrier, inc=1, device_id=peer(d)[1], device_id_type=MESH)
+
+    loads = [
+        pltpu.make_async_copy(src, dst, load_sem.at[i])
+        for i, (src, dst) in enumerate(
+            (
+                (pattern_hbm, pattern_ref),
+                (scale_hbm, scale_ref),
+                (point_hbm, point_ref),
+                (values_hbm, values_ref),
+            )
+        )
+    ]
+    for load in loads:
+        load.start()
+    loads[0].wait()
 
     chosen = [[] for _ in range(SLOTS)]
     count = jnp.int32(0)
@@ -51,6 +66,7 @@
 
     lane = lax.broadcasted_iota(jnp.int32, (1, width), 1)
     signs = jnp.where(lane == 0, 1.0, -1.0).astype(jnp.float32)
+    loads[2].wait()
     point = point_ref[...]
     det = jnp.sum(point * point * signs, axis=1, keepdims=True)
     unit_ref[...] = point / jnp.sqrt(det)
@@ -79,6 +95,8 @@
         barrier, has_left.astype(jnp.int32) + has_right.astype(jnp.int32) + (n_sum - 1)
     )
     send_own(SLOTS)
+    loads[1].wait()
+    loads[3].wait()
     for s in range(SLOTS):
         factor, unit, packed = 0.0, 0.0, None
         for k in range(s, cones):
@@ -195,13 +213,18 @@
         cones, width = cone_point.shape
         strip = rows // n_sum
         vmem = pl.BlockSpec(memory_space=pltpu.VMEM)
-        smem = pl.BlockSpec(memory_space=pltpu.SMEM)
+        hbm = pl.BlockSpec(memory_space=pltpu.HBM)
         return pl.pallas_call(
             functools.partial(kernel, n_tile, n_cone, n_rep),
             out_shape=jax.ShapeDtypeStruct((strip, n_tile * rows), jnp.float32),
-            in_specs=[smem, smem, vmem, vmem],
+            in_specs=[hbm] * 4,
             out_specs=vmem,
             scratch_shapes=[
+                pltpu.SMEM(pattern.shape, jnp.int32),
+                pltpu.SMEM(cone_scale.shape, jnp.float32),
+                pltpu.VMEM(values.shape, jnp.bfloat16),
+                pltpu.VMEM((cones, width), jnp.float32),
+                pltpu.SemaphoreType.DMA((4,)),
                 pltpu.VMEM((cones, width), jnp.float32),
                 pltpu.VMEM((n_tile, SLOTS, rows, width), jnp.bfloat16),
                 pltpu.VMEM((n_tile, 8, width), jnp.int32),

time: 27 us -> 26.5 us (0.981)
  Pallas kernels: 23.2 us -> 22.6 us
    pallas_call x1, Pallas kernels: 23.2 us -> 22.6 us  [per_device(): pl.pallas_call(functools.partial(kernel, n_tile, n_cone, n_rep), out_shap...]
where the time goes in v2:
time: 26.5 us; the launch traced here: 26.3 us
  Pallas kernels  22.6 us (85%)
  local copies, waits for them, and re-layouts  3.63 us (14%)
    pallas_call x1, Pallas kernels, per_device(): pl.pallas_call(functools.partial(kernel, n_tile, n_cone, n_rep), out_shap...  22.6 us
    unnamed x9, local copies, waits for them, and re-layouts  3.63 us

profile of v2, /device:TPU:0, one launch (start us, length us, event | category | flops | bytes accessed | tf_op | source)
XLA Modules:
  0.0 26.3 jit_solution(8699749001423430031)
XLA Ops:
  0.0 0.0 copy-start
  0.0 1.0 %copy-done = bf16[128,1536]{1,0:T(8,128)(2,1)S(1)} copy-done((bf16[128,1536]{1,0:T(8,128)(2,1)S(1)}, bf16[128,1536]{1,0:T(8,128)(2,1)}, u32[]{:S(2)}) %copy-start) | copy-done | bytes 393240
  1.0 0.0 copy-start.1
  1.0 0.7 %copy-done.1 = f32[12,128]{1,0:T(8,128)S(1)} copy-done((f32[12,128]{1,0:T(8,128)S(1)}, f32[12,128]{1,0:T(8,128)}, u32[]{:S(2)}) %copy-start.1) | copy-done | bytes 6168
  1.7 0.0 copy-start.2
  1.7 0.7 %copy-done.2 = s32[1,12]{1,0:T(1,128)S(1)} copy-done((s32[1,12]{1,0:T(1,128)S(1)}, s32[1,12]{1,0:T(1,128)}, u32[]{:S(2)}) %copy-start.2) | copy-done | bytes 72
  2.4 0.0 copy-start.3
  2.4 0.7 %copy-done.3 = f32[12]{0:T(128)S(1)} copy-done((f32[12]{0:T(128)S(1)}, f32[12]{0:T(128)}, u32[]{:S(2)}) %copy-start.3) | copy-done | bytes 72
  3.0 22.6 %shard_map.46 = f32[32,512]{1,0:T(8,128)S(1)} custom-call(s32[1,12]{1,0:T(1,128)S(1)} %copy-done.2, f32[12]{0:T(128)S(1)} %copy-done.3, bf16[128,1536]{1,0:T(8,128)(2,1)S(1)} %copy-done, f32[12,128]{1,0:T(8,128)S(1)} %copy-done.1), custom_call_target="tpu_custom_call" | custom-call | tf_op jit(solution)/shard_map/pallas_call | solution.py:217
  25.7 0.6 %copy.6 = f32[32,512]{1,0:T(8,128)} copy(f32[32,512]{1,0:T(8,128)S(1)} %shard_map.46) | data formatting | bytes 131072
Async XLA Ops:
  0.0 1.0 %copy-start = (bf16[128,1536]{1,0:T(8,128)(2,1)S(1)}, bf16[128,1536]{1,0:T(8,128)(2,1)}, u32[]{:S(2)}) copy-start(bf16[128,1536]{1,0:T(8,128)(2,1)} %values_hbm.1) | copy-start | bytes 1179652
  1.0 0.7 %copy-start.1 = (f32[12,128]{1,0:T(8,128)S(1)}, f32[12,128]{1,0:T(8,128)}, u32[]{:S(2)}) copy-start(f32[12,128]{1,0:T(8,128)} %point_hbm.1) | copy-start | bytes 18436
  1.7 0.7 %copy-start.2 = (s32[1,12]{1,0:T(1,128)S(1)}, s32[1,12]{1,0:T(1,128)}, u32[]{:S(2)}) copy-start(s32[1,12]{1,0:T(1,128)} %pattern_hbm.1) | copy-start | bytes 148
  2.4 0.7 %copy-start.3 = (f32[12]{0:T(128)S(1)}, f32[12]{0:T(128)}, u32[]{:S(2)}) copy-start(f32[12]{0:T(128)} %scale_hbm.1) | copy-start | bytes 148

commit v3 on v2

--- a/solution.py
+++ b/solution.py
@@ -236,7 +236,7 @@
                 pltpu.SemaphoreType.DMA((n_tile, n_sum - 1)),
             ],
             compiler_params=pltpu.CompilerParams(
-                collective_id=0, has_side_effects=True, vmem_limit_bytes=32 * 1024 * 1024
+                collective_id=0, has_side_effects=True, vmem_limit_bytes=60 * 1024 * 1024
             ),
         )(pattern, cone_scale, values, cone_point)
 

time: 26.5 us -> 24.9 us (0.940)
  local copies, waits for them, and re-layouts: 3.63 us -> 1.47 us
  Pallas kernels: 22.6 us -> 23.3 us
    unnamed x9 -> x1, local copies, waits for them, and re-layouts: 3.63 us -> 1.47 us
    pallas_call x1, Pallas kernels: 22.6 us -> 23.3 us  [per_device(): pl.pallas_call(functools.partial(kernel, n_tile, n_cone, n_rep), out_shap...]
where the time goes in v3:
time: 24.9 us; the launch traced here: 24.8 us
  Pallas kernels  23.3 us (94%)
  local copies, waits for them, and re-layouts  1.47 us (6%)
    pallas_call x1, Pallas kernels, per_device(): pl.pallas_call(functools.partial(kernel, n_tile, n_cone, n_rep), out_shap...  23.3 us
    unnamed x1, local copies, waits for them, and re-layouts  1.47 us

profile of v3, /device:TPU:0, one launch (start us, length us, event | category | flops | bytes accessed | tf_op | source)
XLA Modules:
  0.0 24.8 jit_solution(6651023627303261593)
XLA Ops:
  0.0 23.3 %shard_map.46 = f32[32,512]{1,0:T(8,128)} custom-call(s32[1,12]{1,0:T(1,128)} %pattern_hbm.1, f32[12]{0:T(128)} %scale_hbm.1, bf16[128,1536]{1,0:T(8,128)(2,1)} %values_hbm.1, f32[12,128]{1,0:T(8,128)} %point_hbm.1), custom_call_target="tpu_custom_call" | custom-call | tf_op jit(solution)/shard_map/pallas_call | solution.py:217
  23.3 1.5 %copy.6 = f32[32,512]{1,0:T(8,128)} copy(f32[32,512]{1,0:T(8,128)} %shard_map.46) | data formatting | bytes 131072

commit v4 on v1

v4 whole, which is shorter than its diff:
```python
import functools

import jax
import jax.numpy as jnp
from jax import lax
from jax.experimental import pallas as pl
from jax.experimental.pallas import tpu as pltpu
from jax.sharding import PartitionSpec as P

MESH = pl.DeviceIdType.MESH
SLOTS = 6


PARTIAL = jnp.float32


def pack(pattern_ref, scale_ref, values_ref, point_ref, unit_ref, ids_me, held_me, waits, on_ids, on_slot):
    cones, width = point_ref.shape
    waits[0]()
    chosen = [[] for _ in range(SLOTS)]
    count = jnp.int32(0)
    for k in range(cones):
        live = pattern_ref[0, k]
        for s in range(SLOTS):
            chosen[s].append(live * (count == s).astype(jnp.int32) if k >= s else None)
        count = count + live
    for s in range(SLOTS):
        name = sum(chosen[s][k] * (k + 1) for k in range(s, cones))
        ids_me[s : s + 1, :] = jnp.full((1, width), name, jnp.int32)
    on_ids()
    waits[2]()
    lane = lax.broadcasted_iota(jnp.int32, (1, width), 1)
    signs = jnp.where(lane == 0, 1.0, -1.0).astype(jnp.float32)
    point = point_ref[...]
    det = jnp.sum(point * point * signs, axis=1, keepdims=True)
    unit_ref[...] = point / jnp.sqrt(det)
    waits[1]()
    waits[3]()
    for s in range(SLOTS):
        factor, unit, packed = 0.0, 0.0, None
        for k in range(s, cones):
            weight = chosen[s][k].astype(jnp.float32)
            factor = factor + weight * scale_ref[k]
            unit = unit + weight * unit_ref[k : k + 1, :]
            mask = jnp.full((1, width), weight, jnp.float32).astype(jnp.bfloat16)
            term = values_ref[:, k * width : (k + 1) * width] * mask
            packed = term if packed is None else packed + term
        tile = packed.astype(jnp.float32)
        proj = jnp.sum(tile * unit, axis=1, keepdims=True)
        held_me[s] = (factor * (2.0 * proj * unit - tile * signs)).astype(jnp.bfloat16)
        on_slot(s)


def load_all(pairs, load_sem):
    loads = [
        pltpu.make_async_copy(src, dst, load_sem.at[i]) for i, (src, dst) in enumerate(pairs)
    ]
    for load in loads:
        load.start()
    return [load.wait for load in loads]


def matched(first, first_ids, second_ids):
    moved = []
    for b in range(SLOTS):
        total = None
        for a in range(SLOTS):
            same = (first_ids[a : a + 1, :] == second_ids[b : b + 1, :]).astype(jnp.float32)
            term = first[a] * same.astype(jnp.bfloat16)
            total = term if total is None else total + term
        moved.append(total)
    return jnp.concatenate(moved, axis=1)


def wide(ref):
    return jnp.concatenate([ref[s] for s in range(SLOTS)], axis=1)


def outer(x, y):
    return lax.dot_general(
        x, y, (((1,), (1,)), ((), ())), preferred_element_type=jnp.float32
    )


def middle_kernel(n_cone, n_rep, pattern_hbm, scale_hbm, values_hbm, point_hbm, out_ref,
                  pattern_ref, scale_ref, values_ref, point_ref, load_sem, unit_ref, held, ids,
                  own, part, landed, send_sem, recv_sem, part_send, part_recv):
    n_tile = 4
    rows, width = values_ref.shape[0], point_ref.shape[1]
    n_sum = n_cone * n_rep
    strip = rows // n_sum
    me, rep = lax.axis_index("tile"), lax.axis_index("rep")
    here = lax.axis_index("cone") * n_rep + rep
    middle = jnp.logical_or(me == 1, me == 2)
    end = jnp.logical_not(middle)
    twin = n_tile - 1 - me
    near = jnp.where(me < 2, 0, 3)
    far = 3 - near
    heavy = jnp.logical_and(middle, (me == 1) == (rep == 0))
    light = jnp.logical_and(middle, (me == 1) != (rep == 0))

    def place(tile, group):
        return {"tile": tile, "cone": group // n_rep, "rep": lax.rem(group, n_rep)}

    barrier = pltpu.get_barrier_semaphore()
    everyone = n_tile * n_sum
    for d in range(1, everyone):
        other = lax.rem(me * n_sum + here + d, everyone)
        pl.semaphore_signal(
            barrier, inc=1, device_id=place(other // n_sum, lax.rem(other, n_sum)), device_id_type=MESH
        )
    waits = load_all(
        (
            (pattern_hbm, pattern_ref),
            (scale_hbm, scale_ref),
            (point_hbm, point_ref),
            (values_hbm, values_ref),
        ),
        load_sem,
    )

    def block_copy(src, piece):
        ref = ids.at[src] if piece == SLOTS else held.at[src, piece]
        return pltpu.make_async_remote_copy(
            src_ref=ref,
            dst_ref=ref,
            send_sem=send_sem.at[src, piece],
            recv_sem=recv_sem.at[src, piece],
            device_id={"tile": jnp.where(middle, twin, jnp.where(me == 0, 1, 2))},
            device_id_type=MESH,
        )

    def send_own(piece):
        @pl.when(jnp.logical_not(heavy))
        def _():
            block_copy(me, piece).start()

    def on_ids():
        pl.semaphore_wait(barrier, everyone - 1)
        send_own(SLOTS)

    pack(pattern_ref, scale_ref, values_ref, point_ref, unit_ref, ids.at[me], held.at[me], waits, on_ids, send_own)

    def strip_copy(slot, x, y, d):
        group = lax.rem(here + d, n_sum)
        return pltpu.make_async_remote_copy(
            src_ref=part.at[slot, group],
            dst_ref=landed.at[y, here],
            send_sem=part_send.at[slot, group],
            recv_sem=part_recv.at[y, here],
            device_id=place(x, group),
            device_id_type=MESH,
        )

    def share(slot, x, y, block, mine):
        strips = block.reshape(n_sum, strip, width)
        part[slot] = strips.astype(PARTIAL)
        for d in range(1 if mine else 0, n_sum):
            strip_copy(slot, x, y, d).start()
        if mine:
            own[y] = strips

    def pair(slot, x, y, mine):
        left = matched(held[x], ids[x], ids[y])
        right = wide(held.at[y])
        share(slot + 1, y, x, outer(right, left), False)
        share(slot, x, y, outer(left, right), mine)

    def arrive(src):
        for piece in (SLOTS, *range(SLOTS)):
            block_copy(src, piece).wait_recv()

    share(0, me, me, outer(wide(held.at[me]), wide(held.at[me])), True)

    @pl.when(middle)
    def _():
        for piece in (SLOTS, *range(SLOTS)):
            block_copy(near, piece).wait_recv()
            block_copy(near, piece).start()
        pair(1, me, near, True)

        @pl.when(heavy)
        def _():
            arrive(twin)
            pair(3, me, twin, True)

        arrive(far)
        pair(5, me, far, True)

        @pl.when(heavy)
        def _():
            pair(7, near, far, False)

    for y in range(n_tile):
        by_me = jnp.where(middle, jnp.logical_or(y != twin, heavy), y == me)

        def gather(group):
            return pltpu.make_async_remote_copy(
                src_ref=part.at[0, 0],
                dst_ref=landed.at[y, group],
                send_sem=part_send.at[0, 0],
                recv_sem=part_recv.at[y, group],
                device_id=place(twin, group),
                device_id_type=MESH,
            )

        total = None
        for d in range(1, n_sum):
            group = lax.rem(here + d, n_sum)
            gather(group).wait_recv()
            term = landed[y, group].astype(jnp.float32)
            total = term if total is None else total + term

        @pl.when(by_me)
        def _():
            out_ref[:, y * rows : (y + 1) * rows] = total + own[y, here]

        @pl.when(jnp.logical_not(by_me))
        def _():
            gather(here).wait_recv()
            out_ref[:, y * rows : (y + 1) * rows] = total + landed[y, here].astype(jnp.float32)

    def drain_strips(slot, x, mine):
        for d in range(1 if mine else 0, n_sum):
            strip_copy(slot, x, x, d).wait_send()

    @pl.when(jnp.logical_not(heavy))
    def _():
        for piece in range(SLOTS + 1):
            block_copy(me, piece).wait_send()

    drain_strips(0, me, True)

    @pl.when(middle)
    def _():
        for piece in range(SLOTS + 1):
            block_copy(near, piece).wait_send()
        drain_strips(1, me, True)
        drain_strips(2, near, False)
        drain_strips(5, me, True)
        drain_strips(6, far, False)

    @pl.when(heavy)
    def _():
        drain_strips(3, me, True)
        drain_strips(4, twin, False)
        drain_strips(7, near, False)
        drain_strips(8, far, False)


def line_kernel(n_tile, n_cone, n_rep, pattern_hbm, scale_hbm, values_hbm, point_hbm, out_ref,
           pattern_ref, scale_ref, values_ref, point_ref, load_sem, unit_ref, held, ids, part, landed, send_sem, recv_sem, part_send, part_recv):
    rows = values_ref.shape[0]
    cones, width = point_ref.shape
    n_sum = n_cone * n_rep
    strip = rows // n_sum
    me = lax.axis_index("tile")
    here = lax.axis_index("cone") * n_rep + lax.axis_index("rep")
    has_left, has_right = me > 0, me < n_tile - 1

    def peer(d):
        other = lax.rem(here + d, n_sum)
        return other, {"cone": other // n_rep, "rep": lax.rem(other, n_rep)}

    barrier = pltpu.get_barrier_semaphore()

    @pl.when(has_left)
    def _():
        pl.semaphore_signal(barrier, inc=1, device_id={"tile": me - 1}, device_id_type=MESH)

    @pl.when(has_right)
    def _():
        pl.semaphore_signal(barrier, inc=1, device_id={"tile": me + 1}, device_id_type=MESH)

    for d in range(1, n_sum):
        pl.semaphore_signal(barrier, inc=1, device_id=peer(d)[1], device_id_type=MESH)

    waits = load_all(
        (
            (pattern_hbm, pattern_ref),
            (scale_hbm, scale_ref),
            (point_hbm, point_ref),
            (values_hbm, values_ref),
        ),
        load_sem,
    )

    def block_copy(src, piece, right):
        ref = ids.at[src] if piece == SLOTS else held.at[src, piece]
        return pltpu.make_async_remote_copy(
            src_ref=ref,
            dst_ref=ref,
            send_sem=send_sem.at[0 if right else 1, src, piece],
            recv_sem=recv_sem.at[src, piece],
            device_id={"tile": me + 1 if right else me - 1},
            device_id_type=MESH,
        )

    def send_own(piece):
        @pl.when(has_right)
        def _():
            block_copy(me, piece, True).start()

        @pl.when(has_left)
        def _():
            block_copy(me, piece, False).start()

    def on_ids():
        pl.semaphore_wait(
            barrier, has_left.astype(jnp.int32) + has_right.astype(jnp.int32) + (n_sum - 1)
        )
        send_own(SLOTS)

    pack(pattern_ref, scale_ref, values_ref, point_ref, unit_ref, ids.at[me], held.at[me], waits, on_ids, send_own)

    def part_copy(src, d):
        other, device = peer(d)
        return pltpu.make_async_remote_copy(
            src_ref=part.at[src, other],
            dst_ref=landed.at[src, d - 1],
            send_sem=part_send.at[src, d - 1],
            recv_sem=part_recv.at[src, d - 1],
            device_id=device,
            device_id_type=MESH,
        )

    def product(src, own):
        left = wide(held.at[me]) if own else matched(held[me], ids[me], ids[src])
        block = outer(left, wide(held.at[src]))
        part[src] = block.reshape(n_sum, strip, width)
        for d in range(1, n_sum):
            part_copy(src, d).start()

    product(me, True)

    def step(s, carry):
        from_left, from_right = me - s, me + s
        for piece in (SLOTS, *range(SLOTS)):
            @pl.when(from_left >= 0)
            def _():
                block_copy(from_left, piece, True).wait_recv()

                @pl.when(has_right)
                def _():
                    block_copy(from_left, piece, True).start()

            @pl.when(from_right < n_tile)
            def _():
                block_copy(from_right, piece, False).wait_recv()

                @pl.when(has_left)
                def _():
                    block_copy(from_right, piece, False).start()

        @pl.when(from_left >= 0)
        def _():
            product(from_left, False)

        @pl.when(from_right < n_tile)
        def _():
            product(from_right, False)

        return carry

    lax.fori_loop(1, n_tile, step, 0)

    for src in range(n_tile):
        total = part[src, here]
        for d in range(1, n_sum):
            part_copy(src, d).wait_recv()
            total = total + landed[src, d - 1]
        out_ref[:, src * rows : (src + 1) * rows] = total

    def drain(src, carry):
        for d in range(1, n_sum):
            part_copy(src, d).wait_send()

        @pl.when(jnp.logical_and(has_right, src <= me))
        def _():
            for piece in range(SLOTS + 1):
                block_copy(src, piece, True).wait_send()

        @pl.when(jnp.logical_and(has_left, src >= me))
        def _():
            for piece in range(SLOTS + 1):
                block_copy(src, piece, False).wait_send()

        return carry

    lax.fori_loop(0, n_tile, drain, 0)


def solution(mesh):
    n_tile, n_cone, n_rep = mesh.shape["tile"], mesh.shape["cone"], mesh.shape["rep"]
    n_sum = n_cone * n_rep

    def per_device(values, pattern, cone_point, cone_scale):
        rows, cols = values.shape
        cones, width = cone_point.shape
        strip = rows // n_sum
        vmem = pl.BlockSpec(memory_space=pltpu.VMEM)
        hbm = pl.BlockSpec(memory_space=pltpu.HBM)
        loads = [
            pltpu.SMEM(pattern.shape, jnp.int32),
            pltpu.SMEM(cone_scale.shape, jnp.float32),
            pltpu.VMEM(values.shape, jnp.bfloat16),
            pltpu.VMEM((cones, width), jnp.float32),
            pltpu.SemaphoreType.DMA((4,)),
            pltpu.VMEM((cones, width), jnp.float32),
            pltpu.VMEM((n_tile, SLOTS, rows, width), jnp.bfloat16),
            pltpu.VMEM((n_tile, 8, width), jnp.int32),
        ]
        if n_tile == 4 and n_rep == 2:
            body = functools.partial(middle_kernel, n_cone, n_rep)
            scratch = [
                pltpu.VMEM((n_tile, n_sum, strip, rows), jnp.float32),
                pltpu.VMEM((9, n_sum, strip, rows), PARTIAL),
                pltpu.VMEM((n_tile, n_sum, strip, rows), PARTIAL),
                pltpu.SemaphoreType.DMA((n_tile, SLOTS + 1)),
                pltpu.SemaphoreType.DMA((n_tile, SLOTS + 1)),
                pltpu.SemaphoreType.DMA((9, n_sum)),
                pltpu.SemaphoreType.DMA((n_tile, n_sum)),
            ]
        else:
            body = functools.partial(line_kernel, n_tile, n_cone, n_rep)
            scratch = [
                pltpu.VMEM((n_tile, n_sum, strip, rows), jnp.float32),
                pltpu.VMEM((n_tile, n_sum - 1, strip, rows), jnp.float32),
                pltpu.SemaphoreType.DMA((2, n_tile, SLOTS + 1)),
                pltpu.SemaphoreType.DMA((n_tile, SLOTS + 1)),
                pltpu.SemaphoreType.DMA((n_tile, n_sum - 1)),
                pltpu.SemaphoreType.DMA((n_tile, n_sum - 1)),
            ]
        return pl.pallas_call(
            body,
            out_shape=jax.ShapeDtypeStruct((strip, n_tile * rows), jnp.float32),
            in_specs=[hbm] * 4,
            out_specs=vmem,
            scratch_shapes=loads + scratch,
            compiler_params=pltpu.CompilerParams(
                collective_id=0, has_side_effects=True, vmem_limit_bytes=60 * 1024 * 1024
            ),
        )(pattern, cone_scale, values, cone_point)

    return jax.shard_map(
        per_device,
        mesh=mesh,
        in_specs=(
            P(("groups", "tile"), ("cone", "rep")),
            P(("groups", "tile"), ("cone", "rep")),
            P(("groups", "cone", "rep"), None),
            P(("groups", "cone", "rep")),
        ),
        out_specs=P(("groups", "tile", "cone", "rep"), None),
        check_vma=False,
    )
```

time: 27 us -> 23.4 us (0.87)
  local copies, waits for them, and re-layouts: 3.63 us -> 1.47 us
  Pallas kernels: 23.2 us -> 21.8 us
    unnamed x9 -> x1, local copies, waits for them, and re-layouts: 3.63 us -> 1.47 us
    pallas_call x1, Pallas kernels: 23.2 us -> 21.8 us  [per_device(): pl.pallas_call(body, out_shape=jax.ShapeDtypeStruct((strip, n_tile * rows...]
where the time goes in v4:
time: 23.4 us; the launch traced here: 23.3 us
  Pallas kernels  21.8 us (93%)
  local copies, waits for them, and re-layouts  1.47 us (6%)
    pallas_call x1, Pallas kernels, per_device(): pl.pallas_call(body, out_shape=jax.ShapeDtypeStruct((strip, n_tile * rows...  21.8 us
    unnamed x1, local copies, waits for them, and re-layouts  1.47 us

profile of v4, /device:TPU:0, one launch (start us, length us, event | category | flops | bytes accessed | tf_op | source)
XLA Modules:
  0.0 23.3 jit_solution(80730728711625788)
XLA Ops:
  0.0 21.8 %shard_map.46 = f32[32,512]{1,0:T(8,128)} custom-call(s32[1,12]{1,0:T(1,128)} %pattern_hbm.1, f32[12]{0:T(128)} %scale_hbm.1, bf16[128,1536]{1,0:T(8,128)(2,1)} %values_hbm.1, f32[12,128]{1,0:T(8,128)} %point_hbm.1), custom_call_target="tpu_custom_call" | custom-call | tf_op jit(solution)/shard_map/pallas_call | solution.py:434
  21.8 1.5 %copy.6 = f32[32,512]{1,0:T(8,128)} copy(f32[32,512]{1,0:T(8,128)} %shard_map.46) | data formatting | bytes 131072

commit v5 on v4

--- a/solution.py
+++ b/solution.py
@@ -11,7 +11,7 @@
 SLOTS = 6
 
 
-PARTIAL = jnp.float32
+PARTIAL = jnp.bfloat16
 
 
 def pack(pattern_ref, scale_ref, values_ref, point_ref, unit_ref, ids_me, held_me, waits, on_ids, on_slot):
@@ -172,27 +172,26 @@
 
     share(0, me, me, outer(wide(held.at[me]), wide(held.at[me])), True)
 
-    @pl.when(middle)
+    @pl.when(light)
     def _():
         for piece in (SLOTS, *range(SLOTS)):
             block_copy(near, piece).wait_recv()
             block_copy(near, piece).start()
         pair(1, me, near, True)
 
-        @pl.when(heavy)
-        def _():
-            arrive(twin)
-            pair(3, me, twin, True)
-
+    @pl.when(heavy)
+    def _():
+        arrive(twin)
+        pair(3, me, twin, True)
+        arrive(near)
+        pair(1, me, near, True)
+        pair(5, near, twin, False)
         arrive(far)
-        pair(5, me, far, True)
-
-        @pl.when(heavy)
-        def _():
-            pair(7, near, far, False)
+        pair(7, me, far, True)
+        pair(9, near, far, False)
 
     for y in range(n_tile):
-        by_me = jnp.where(middle, jnp.logical_or(y != twin, heavy), y == me)
+        by_me = jnp.logical_or(heavy, jnp.logical_or(y == me, jnp.logical_and(light, y == near)))
 
         def gather(group):
             return pltpu.make_async_remote_copy(
@@ -233,19 +232,24 @@
 
     @pl.when(middle)
     def _():
+        drain_strips(1, me, True)
+        drain_strips(2, near, False)
+
+    @pl.when(light)
+    def _():
         for piece in range(SLOTS + 1):
             block_copy(near, piece).wait_send()
-        drain_strips(1, me, True)
-        drain_strips(2, near, False)
-        drain_strips(5, me, True)
-        drain_strips(6, far, False)
 
     @pl.when(heavy)
     def _():
         drain_strips(3, me, True)
         drain_strips(4, twin, False)
-        drain_strips(7, near, False)
+        drain_strips(5, near, False)
+        drain_strips(6, twin, False)
+        drain_strips(7, me, True)
         drain_strips(8, far, False)
+        drain_strips(9, near, False)
+        drain_strips(10, far, False)
 
 
 def line_kernel(n_tile, n_cone, n_rep, pattern_hbm, scale_hbm, values_hbm, point_hbm, out_ref,
@@ -414,11 +418,11 @@
             body = functools.partial(middle_kernel, n_cone, n_rep)
             scratch = [
                 pltpu.VMEM((n_tile, n_sum, strip, rows), jnp.float32),
-                pltpu.VMEM((9, n_sum, strip, rows), PARTIAL),
+                pltpu.VMEM((11, n_sum, strip, rows), PARTIAL),
                 pltpu.VMEM((n_tile, n_sum, strip, rows), PARTIAL),
                 pltpu.SemaphoreType.DMA((n_tile, SLOTS + 1)),
                 pltpu.SemaphoreType.DMA((n_tile, SLOTS + 1)),
-                pltpu.SemaphoreType.DMA((9, n_sum)),
+                pltpu.SemaphoreType.DMA((11, n_sum)),
                 pltpu.SemaphoreType.DMA((n_tile, n_sum)),
             ]
         else:
@@ -433,7 +437,7 @@
             ]
         return pl.pallas_call(
             body,
-            out_shape=jax.ShapeDtypeStruct((strip, n_tile * rows), jnp.float32),
+            out_shape=pltpu.VMEM((strip, n_tile * rows), jnp.float32),
             in_specs=[hbm] * 4,
             out_specs=vmem,
             scratch_shapes=loads + scratch,

time: 23.4 us -> 20 us (0.85)
  Pallas kernels: 21.8 us -> 19.2 us
  local copies, waits for them, and re-layouts: 1.47 us -> 0.63 us
    pallas_call x1, Pallas kernels: 21.8 us -> 19.2 us  [per_device(): pl.pallas_call(body, out_shape=pltpu.VMEM((strip, n_tile * rows), jnp.flo...]
    unnamed x1, local copies, waits for them, and re-layouts: 1.47 us -> 0.63 us
where the time goes in v5:
time: 20 us; the launch traced here: 19.9 us
  Pallas kernels  19.2 us (96%)
  local copies, waits for them, and re-layouts  0.63 us (3%)
    pallas_call x1, Pallas kernels, per_device(): pl.pallas_call(body, out_shape=pltpu.VMEM((strip, n_tile * rows), jnp.flo...  19.2 us
    unnamed x1, local copies, waits for them, and re-layouts  0.63 us

profile of v5, /device:TPU:0, one launch (start us, length us, event | category | flops | bytes accessed | tf_op | source)
XLA Modules:
  0.0 19.9 jit_solution(3166590418582699975)
XLA Ops:
  0.0 19.2 %shard_map.46 = f32[32,512]{1,0:T(8,128)S(1)} custom-call(s32[1,12]{1,0:T(1,128)} %pattern_hbm.1, f32[12]{0:T(128)} %scale_hbm.1, bf16[128,1536]{1,0:T(8,128)(2,1)} %values_hbm.1, f32[12,128]{1,0:T(8,128)} %point_hbm.1), custom_call_target="tpu_custom_call" | custom-call | tf_op jit(solution)/shard_map/pallas_call | solution.py:438
  19.2 0.6 %copy.6 = f32[32,512]{1,0:T(8,128)} copy(f32[32,512]{1,0:T(8,128)S(1)} %shard_map.46) | data formatting | bytes 131072

commit v6 on v4

--- a/solution.py
+++ b/solution.py
@@ -11,10 +11,10 @@
 SLOTS = 6
 
 
-PARTIAL = jnp.float32
-
-
-def pack(pattern_ref, scale_ref, values_ref, point_ref, unit_ref, ids_me, held_me, waits, on_ids, on_slot):
+PARTIAL = jnp.bfloat16
+
+
+def pack(pattern_ref, scale_ref, values_ref, point_ref, unit_ref, ids_me, held_me, waits, on_ids, on_strip):
     cones, width = point_ref.shape
     waits[0]()
     chosen = [[] for _ in range(SLOTS)]
@@ -36,19 +36,26 @@
     unit_ref[...] = point / jnp.sqrt(det)
     waits[1]()
     waits[3]()
+    slots = []
     for s in range(SLOTS):
-        factor, unit, packed = 0.0, 0.0, None
+        factor, unit, masks = 0.0, 0.0, []
         for k in range(s, cones):
             weight = chosen[s][k].astype(jnp.float32)
             factor = factor + weight * scale_ref[k]
             unit = unit + weight * unit_ref[k : k + 1, :]
-            mask = jnp.full((1, width), weight, jnp.float32).astype(jnp.bfloat16)
-            term = values_ref[:, k * width : (k + 1) * width] * mask
-            packed = term if packed is None else packed + term
-        tile = packed.astype(jnp.float32)
-        proj = jnp.sum(tile * unit, axis=1, keepdims=True)
-        held_me[s] = (factor * (2.0 * proj * unit - tile * signs)).astype(jnp.bfloat16)
-        on_slot(s)
+            masks.append(jnp.full((1, width), weight, jnp.float32).astype(jnp.bfloat16))
+        slots.append((factor, unit, masks))
+    strip = held_me.shape[2]
+    for q in range(held_me.shape[0]):
+        for s, (factor, unit, masks) in enumerate(slots):
+            packed = None
+            for k, mask in zip(range(s, cones), masks):
+                term = values_ref[q * strip : (q + 1) * strip, k * width : (k + 1) * width] * mask
+                packed = term if packed is None else packed + term
+            tile = packed.astype(jnp.float32)
+            proj = jnp.sum(tile * unit, axis=1, keepdims=True)
+            held_me[q, s] = (factor * (2.0 * proj * unit - tile * signs)).astype(jnp.bfloat16)
+        on_strip(q)
 
 
 def load_all(pairs, load_sem):
@@ -60,20 +67,25 @@
     return [load.wait for load in loads]
 
 
+def slots_of(ref):
+    return [ref[:, s].reshape(-1, ref.shape[3]) for s in range(SLOTS)]
+
+
+def wide(ref):
+    return jnp.concatenate(slots_of(ref), axis=1)
+
+
 def matched(first, first_ids, second_ids):
     moved = []
+    tiles = slots_of(first)
     for b in range(SLOTS):
         total = None
         for a in range(SLOTS):
             same = (first_ids[a : a + 1, :] == second_ids[b : b + 1, :]).astype(jnp.float32)
-            term = first[a] * same.astype(jnp.bfloat16)
+            term = tiles[a] * same.astype(jnp.bfloat16)
             total = term if total is None else total + term
         moved.append(total)
     return jnp.concatenate(moved, axis=1)
-
-
-def wide(ref):
-    return jnp.concatenate([ref[s] for s in range(SLOTS)], axis=1)
 
 
 def outer(x, y):
@@ -91,24 +103,12 @@
     strip = rows // n_sum
     me, rep = lax.axis_index("tile"), lax.axis_index("rep")
     here = lax.axis_index("cone") * n_rep + rep
-    middle = jnp.logical_or(me == 1, me == 2)
-    end = jnp.logical_not(middle)
-    twin = n_tile - 1 - me
-    near = jnp.where(me < 2, 0, 3)
+    heavy_tile = 1 + rep
+    heavy = me == heavy_tile
+    twin = 3 - heavy_tile
+    near = 3 * rep
     far = 3 - near
-    heavy = jnp.logical_and(middle, (me == 1) == (rep == 0))
-    light = jnp.logical_and(middle, (me == 1) != (rep == 0))
-
-    def place(tile, group):
-        return {"tile": tile, "cone": group // n_rep, "rep": lax.rem(group, n_rep)}
-
-    barrier = pltpu.get_barrier_semaphore()
-    everyone = n_tile * n_sum
-    for d in range(1, everyone):
-        other = lax.rem(me * n_sum + here + d, everyone)
-        pl.semaphore_signal(
-            barrier, inc=1, device_id=place(other // n_sum, lax.rem(other, n_sum)), device_id_type=MESH
-        )
+
     waits = load_all(
         (
             (pattern_hbm, pattern_ref),
@@ -119,14 +119,25 @@
         load_sem,
     )
 
+    def place(tile, group):
+        return {"tile": tile, "cone": group // n_rep, "rep": lax.rem(group, n_rep)}
+
+    barrier = pltpu.get_barrier_semaphore()
+    everyone = n_tile * n_sum
+    for d in range(1, everyone):
+        other = lax.rem(me * n_sum + here + d, everyone)
+        pl.semaphore_signal(
+            barrier, inc=1, device_id=place(other // n_sum, lax.rem(other, n_sum)), device_id_type=MESH
+        )
+
     def block_copy(src, piece):
-        ref = ids.at[src] if piece == SLOTS else held.at[src, piece]
+        ref = ids.at[src] if piece == n_sum else held.at[src, piece]
         return pltpu.make_async_remote_copy(
             src_ref=ref,
             dst_ref=ref,
             send_sem=send_sem.at[src, piece],
             recv_sem=recv_sem.at[src, piece],
-            device_id={"tile": jnp.where(middle, twin, jnp.where(me == 0, 1, 2))},
+            device_id={"tile": heavy_tile},
             device_id_type=MESH,
         )
 
@@ -137,78 +148,140 @@
 
     def on_ids():
         pl.semaphore_wait(barrier, everyone - 1)
-        send_own(SLOTS)
+        send_own(n_sum)
 
     pack(pattern_ref, scale_ref, values_ref, point_ref, unit_ref, ids.at[me], held.at[me], waits, on_ids, send_own)
 
-    def strip_copy(slot, x, y, d):
-        group = lax.rem(here + d, n_sum)
+    def strip_copy(slot, x, y, group, count=1):
         return pltpu.make_async_remote_copy(
-            src_ref=part.at[slot, group],
-            dst_ref=landed.at[y, here],
+            src_ref=part.at[pl.ds(slot, count), group],
+            dst_ref=landed.at[pl.ds(y, count), here],
             send_sem=part_send.at[slot, group],
             recv_sem=part_recv.at[y, here],
             device_id=place(x, group),
             device_id_type=MESH,
         )
 
-    def share(slot, x, y, block, mine):
+    def send(slot, x, y, mine, count=1):
+        for d in range(1 if mine else 0, n_sum):
+            strip_copy(slot, x, y, lax.rem(here + d, n_sum), count).start()
+
+    def drain(slot, x, y, mine, count=1):
+        for d in range(1 if mine else 0, n_sum):
+            strip_copy(slot, x, y, lax.rem(here + d, n_sum), count).wait_send()
+
+    def put(slot, block, y=None):
         strips = block.reshape(n_sum, strip, width)
         part[slot] = strips.astype(PARTIAL)
-        for d in range(1 if mine else 0, n_sum):
-            strip_copy(slot, x, y, d).start()
-        if mine:
+        if y is not None:
             own[y] = strips
 
-    def pair(slot, x, y, mine):
-        left = matched(held[x], ids[x], ids[y])
-        right = wide(held.at[y])
-        share(slot + 1, y, x, outer(right, left), False)
-        share(slot, x, y, outer(left, right), mine)
-
-    def arrive(src):
-        for piece in (SLOTS, *range(SLOTS)):
-            block_copy(src, piece).wait_recv()
-
-    share(0, me, me, outer(wide(held.at[me]), wide(held.at[me])), True)
-
-    @pl.when(middle)
+    def arrive(src, piece):
+        block_copy(src, piece).wait_recv()
+
+    def moved(blocks, to):
+        return jnp.concatenate([matched(held.at[x], ids[x], ids[to]) for x in blocks], axis=0)
+
+    low = heavy_tile - 1
+    diagonal_send = (0, me, me, True, 1)
+    twin_sends = ((0, me, 1, True, 2), (2, twin, me, False, 1))
+    near_send = (4, near, 1, False, 2)
+    near_sends = ((3, twin, near, False, 1), (7, me, near, True, 1))
+    far_send = (9, far, low, False, 3)
+    far_sends = ((6, near, far, False, 1), (12, twin, far, False, 1), (8, me, far, True, 1))
+
+    put(jnp.where(heavy, low, 0), outer(wide(held.at[me]), wide(held.at[me])), me)
+
+    @pl.when(jnp.logical_not(heavy))
     def _():
-        for piece in (SLOTS, *range(SLOTS)):
-            block_copy(near, piece).wait_recv()
-            block_copy(near, piece).start()
-        pair(1, me, near, True)
-
-        @pl.when(heavy)
-        def _():
-            arrive(twin)
-            pair(3, me, twin, True)
-
-        arrive(far)
-        pair(5, me, far, True)
-
-        @pl.when(heavy)
-        def _():
-            pair(7, near, far, False)
+        send(*diagonal_send)
+
+    @pl.when(heavy)
+    def _():
+        for piece in (n_sum, *range(n_sum)):
+            arrive(twin, piece)
+        left, right = moved((me,), twin), wide(held.at[twin])
+        put(2, outer(right, left))
+        put(twin - 1, outer(left, right), twin)
+        for message in twin_sends:
+            send(*message)
+
+        arrive(near, n_sum)
+        left = moved((me, twin), near)
+        for q in range(n_sum):
+            arrive(near, q)
+        right = wide(held.at[near])
+        block = outer(right, left)
+        put(4 + me - 1, block[:, :width])
+        put(4 + twin - 1, block[:, width:])
+        send(*near_send)
+        block = outer(left, right)
+        put(7, block[:rows], near)
+        put(3, block[rows:])
+        for message in near_sends:
+            send(*message)
+
+        arrive(far, n_sum)
+        left = moved((me, near, twin), far)
+        for q in range(n_sum):
+            arrive(far, q)
+        right = wide(held.at[far])
+        block = outer(right, left)
+        put(9 + me - low, block[:, :width])
+        put(9 + near - low, block[:, width : 2 * width])
+        put(9 + twin - low, block[:, 2 * width :])
+        send(*far_send)
+        block = outer(left, right)
+        put(8, block[:rows], far)
+        put(6, block[rows : 2 * rows])
+        put(12, block[2 * rows :])
+        for message in far_sends:
+            send(*message)
+
+    def expect(y, group, count=1):
+        pltpu.make_async_remote_copy(
+            src_ref=part.at[pl.ds(0, count), 0],
+            dst_ref=landed.at[pl.ds(y, count), group],
+            send_sem=part_send.at[0, 0],
+            recv_sem=part_recv.at[y, group],
+            device_id=place(lax.rem(me + 1, n_tile), group),
+            device_id_type=MESH,
+        ).wait_recv()
+
+    for group in range(n_sum):
+        h, n = 1 + group % n_rep, 3 * (group % n_rep)
+        l, f = 3 - h, 3 - n
+
+        @pl.when(jnp.logical_and(me == h, here != group))
+        def _():
+            expect(1, group, 2)
+            expect(n, group)
+            expect(f, group)
+
+        @pl.when(me == l)
+        def _():
+            expect(h, group)
+            expect(n, group)
+            expect(f, group)
+
+        @pl.when(me == n)
+        def _():
+            expect(1, group, 2)
+            expect(f, group)
+
+        @pl.when(me == f)
+        def _():
+            expect(h - 1, group, 3)
+
+        @pl.when(jnp.logical_and(me != h, here != group))
+        def _():
+            expect(me, group)
 
     for y in range(n_tile):
-        by_me = jnp.where(middle, jnp.logical_or(y != twin, heavy), y == me)
-
-        def gather(group):
-            return pltpu.make_async_remote_copy(
-                src_ref=part.at[0, 0],
-                dst_ref=landed.at[y, group],
-                send_sem=part_send.at[0, 0],
-                recv_sem=part_recv.at[y, group],
-                device_id=place(twin, group),
-                device_id_type=MESH,
-            )
-
+        by_me = jnp.logical_or(heavy, y == me)
         total = None
         for d in range(1, n_sum):
-            group = lax.rem(here + d, n_sum)
-            gather(group).wait_recv()
-            term = landed[y, group].astype(jnp.float32)
+            term = landed[y, lax.rem(here + d, n_sum)].astype(jnp.float32)
             total = term if total is None else total + term
 
         @pl.when(by_me)
@@ -217,35 +290,18 @@
 
         @pl.when(jnp.logical_not(by_me))
         def _():
-            gather(here).wait_recv()
             out_ref[:, y * rows : (y + 1) * rows] = total + landed[y, here].astype(jnp.float32)
-
-    def drain_strips(slot, x, mine):
-        for d in range(1 if mine else 0, n_sum):
-            strip_copy(slot, x, x, d).wait_send()
 
     @pl.when(jnp.logical_not(heavy))
     def _():
-        for piece in range(SLOTS + 1):
+        for piece in range(n_sum + 1):
             block_copy(me, piece).wait_send()
-
-    drain_strips(0, me, True)
-
-    @pl.when(middle)
-    def _():
-        for piece in range(SLOTS + 1):
-            block_copy(near, piece).wait_send()
-        drain_strips(1, me, True)
-        drain_strips(2, near, False)
-        drain_strips(5, me, True)
-        drain_strips(6, far, False)
+        drain(*diagonal_send)
 
     @pl.when(heavy)
     def _():
-        drain_strips(3, me, True)
-        drain_strips(4, twin, False)
-        drain_strips(7, near, False)
-        drain_strips(8, far, False)
+        for message in (*twin_sends, near_send, *near_sends, far_send, *far_sends):
+            drain(*message)
 
 
 def line_kernel(n_tile, n_cone, n_rep, pattern_hbm, scale_hbm, values_hbm, point_hbm, out_ref,
@@ -286,7 +342,7 @@
     )
 
     def block_copy(src, piece, right):
-        ref = ids.at[src] if piece == SLOTS else held.at[src, piece]
+        ref = ids.at[src] if piece == n_sum else held.at[src, piece]
         return pltpu.make_async_remote_copy(
             src_ref=ref,
             dst_ref=ref,
@@ -309,7 +365,7 @@
         pl.semaphore_wait(
             barrier, has_left.astype(jnp.int32) + has_right.astype(jnp.int32) + (n_sum - 1)
         )
-        send_own(SLOTS)
+        send_own(n_sum)
 
     pack(pattern_ref, scale_ref, values_ref, point_ref, unit_ref, ids.at[me], held.at[me], waits, on_ids, send_own)
 
@@ -325,7 +381,7 @@
         )
 
     def product(src, own):
-        left = wide(held.at[me]) if own else matched(held[me], ids[me], ids[src])
+        left = wide(held.at[me]) if own else matched(held.at[me], ids[me], ids[src])
         block = outer(left, wide(held.at[src]))
         part[src] = block.reshape(n_sum, strip, width)
         for d in range(1, n_sum):
@@ -335,7 +391,7 @@
 
     def step(s, carry):
         from_left, from_right = me - s, me + s
-        for piece in (SLOTS, *range(SLOTS)):
+        for piece in (n_sum, *range(n_sum)):
             @pl.when(from_left >= 0)
             def _():
                 block_copy(from_left, piece, True).wait_recv()
@@ -377,12 +433,12 @@
 
         @pl.when(jnp.logical_and(has_right, src <= me))
         def _():
-            for piece in range(SLOTS + 1):
+            for piece in range(n_sum + 1):
                 block_copy(src, piece, True).wait_send()
 
         @pl.when(jnp.logical_and(has_left, src >= me))
         def _():
-            for piece in range(SLOTS + 1):
+            for piece in range(n_sum + 1):
                 block_copy(src, piece, False).wait_send()
 
         return carry
@@ -407,18 +463,18 @@
             pltpu.VMEM((cones, width), jnp.float32),
             pltpu.SemaphoreType.DMA((4,)),
             pltpu.VMEM((cones, width), jnp.float32),
-            pltpu.VMEM((n_tile, SLOTS, rows, width), jnp.bfloat16),
+            pltpu.VMEM((n_tile, n_sum, SLOTS, strip, width), jnp.bfloat16),
             pltpu.VMEM((n_tile, 8, width), jnp.int32),
         ]
         if n_tile == 4 and n_rep == 2:
             body = functools.partial(middle_kernel, n_cone, n_rep)
             scratch = [
                 pltpu.VMEM((n_tile, n_sum, strip, rows), jnp.float32),
-                pltpu.VMEM((9, n_sum, strip, rows), PARTIAL),
+                pltpu.VMEM((13, n_sum, strip, rows), PARTIAL),
                 pltpu.VMEM((n_tile, n_sum, strip, rows), PARTIAL),
-                pltpu.SemaphoreType.DMA((n_tile, SLOTS + 1)),
-                pltpu.SemaphoreType.DMA((n_tile, SLOTS + 1)),
-                pltpu.SemaphoreType.DMA((9, n_sum)),
+                pltpu.SemaphoreType.DMA((n_tile, n_sum + 1)),
+                pltpu.SemaphoreType.DMA((n_tile, n_sum + 1)),
+                pltpu.SemaphoreType.DMA((13, n_sum)),
                 pltpu.SemaphoreType.DMA((n_tile, n_sum)),
             ]
         else:
@@ -426,14 +482,14 @@
             scratch = [
                 pltpu.VMEM((n_tile, n_sum, strip, rows), jnp.float32),
                 pltpu.VMEM((n_tile, n_sum - 1, strip, rows), jnp.float32),
-                pltpu.SemaphoreType.DMA((2, n_tile, SLOTS + 1)),
-                pltpu.SemaphoreType.DMA((n_tile, SLOTS + 1)),
+                pltpu.SemaphoreType.DMA((2, n_tile, n_sum + 1)),
+                pltpu.SemaphoreType.DMA((n_tile, n_sum + 1)),
                 pltpu.SemaphoreType.DMA((n_tile, n_sum - 1)),
                 pltpu.SemaphoreType.DMA((n_tile, n_sum - 1)),
             ]
         return pl.pallas_call(
             body,
-            out_shape=jax.ShapeDtypeStruct((strip, n_tile * rows), jnp.float32),
+            out_shape=pltpu.VMEM((strip, n_tile * rows), jnp.float32),
             in_specs=[hbm] * 4,
             out_specs=vmem,
             scratch_shapes=loads + scratch,

time: 23.4 us -> 19.9 us (0.85)
  Pallas kernels: 21.8 us -> 19.1 us
  local copies, waits for them, and re-layouts: 1.47 us -> 0.63 us
    pallas_call x1, Pallas kernels: 21.8 us -> 19.1 us  [per_device(): pl.pallas_call(body, out_shape=pltpu.VMEM((strip, n_tile * rows), jnp.flo...]
    unnamed x1, local copies, waits for them, and re-layouts: 1.47 us -> 0.63 us
where the time goes in v6:
time: 19.9 us; the launch traced here: 19.7 us
  Pallas kernels  19.1 us (96%)
  local copies, waits for them, and re-layouts  0.63 us (3%)
    pallas_call x1, Pallas kernels, per_device(): pl.pallas_call(body, out_shape=pltpu.VMEM((strip, n_tile * rows), jnp.flo...  19.1 us
    unnamed x1, local copies, waits for them, and re-layouts  0.63 us

profile of v6, /device:TPU:0, one launch (start us, length us, event | category | flops | bytes accessed | tf_op | source)
XLA Modules:
  0.0 19.7 jit_solution(2371777916896118169)
XLA Ops:
  0.0 19.1 %shard_map.46 = f32[32,512]{1,0:T(8,128)S(1)} custom-call(s32[1,12]{1,0:T(1,128)} %pattern_hbm.1, f32[12]{0:T(128)} %scale_hbm.1, bf16[128,1536]{1,0:T(8,128)(2,1)} %values_hbm.1, f32[12,128]{1,0:T(8,128)} %point_hbm.1), custom_call_target="tpu_custom_call" | custom-call | tf_op jit(solution)/shard_map/pallas_call | solution.py:490
  19.1 0.6 %copy.6 = f32[32,512]{1,0:T(8,128)} copy(f32[32,512]{1,0:T(8,128)S(1)} %shard_map.46) | data formatting | bytes 131072

commit v7 on v6

--- a/solution.py
+++ b/solution.py
@@ -35,7 +35,6 @@
     det = jnp.sum(point * point * signs, axis=1, keepdims=True)
     unit_ref[...] = point / jnp.sqrt(det)
     waits[1]()
-    waits[3]()
     slots = []
     for s in range(SLOTS):
         factor, unit, masks = 0.0, 0.0, []
@@ -47,6 +46,7 @@
         slots.append((factor, unit, masks))
     strip = held_me.shape[2]
     for q in range(held_me.shape[0]):
+        waits[3 + q]()
         for s, (factor, unit, masks) in enumerate(slots):
             packed = None
             for k, mask in zip(range(s, cones), masks):
@@ -96,7 +96,7 @@
 
 def middle_kernel(n_cone, n_rep, pattern_hbm, scale_hbm, values_hbm, point_hbm, out_ref,
                   pattern_ref, scale_ref, values_ref, point_ref, load_sem, unit_ref, held, ids,
-                  own, part, landed, send_sem, recv_sem, part_send, part_recv):
+                  own, part, landed, send_sem, recv_sem, part_send, part_recv, turn):
     n_tile = 4
     rows, width = values_ref.shape[0], point_ref.shape[1]
     n_sum = n_cone * n_rep
@@ -114,7 +114,10 @@
             (pattern_hbm, pattern_ref),
             (scale_hbm, scale_ref),
             (point_hbm, point_ref),
-            (values_hbm, values_ref),
+            *(
+                (values_hbm.at[pl.ds(q * strip, strip)], values_ref.at[pl.ds(q * strip, strip)])
+                for q in range(n_sum)
+            ),
         ),
         load_sem,
     )
@@ -142,7 +145,7 @@
         )
 
     def send_own(piece):
-        @pl.when(jnp.logical_not(heavy))
+        @pl.when(jnp.logical_not(heavy) if piece == n_sum else jnp.logical_or(me == near, me == twin))
         def _():
             block_copy(me, piece).start()
 
@@ -151,6 +154,17 @@
         send_own(n_sum)
 
     pack(pattern_ref, scale_ref, values_ref, point_ref, unit_ref, ids.at[me], held.at[me], waits, on_ids, send_own)
+
+    @pl.when(me == near)
+    def _():
+        block_copy(me, n_sum // 2).wait_send()
+        pl.semaphore_signal(turn, inc=1, device_id={"rep": 1 - rep}, device_id_type=MESH)
+
+    @pl.when(me == far)
+    def _():
+        pl.semaphore_wait(turn, 1)
+        for piece in range(n_sum):
+            block_copy(me, piece).start()
 
     def strip_copy(slot, x, y, group, count=1):
         return pltpu.make_async_remote_copy(
@@ -295,8 +309,13 @@
     @pl.when(jnp.logical_not(heavy))
     def _():
         for piece in range(n_sum + 1):
-            block_copy(me, piece).wait_send()
+            if piece != n_sum // 2:
+                block_copy(me, piece).wait_send()
         drain(*diagonal_send)
+
+    @pl.when(jnp.logical_or(me == far, me == twin))
+    def _():
+        block_copy(me, n_sum // 2).wait_send()
 
     @pl.when(heavy)
     def _():
@@ -336,7 +355,10 @@
             (pattern_hbm, pattern_ref),
             (scale_hbm, scale_ref),
             (point_hbm, point_ref),
-            (values_hbm, values_ref),
+            *(
+                (values_hbm.at[pl.ds(q * strip, strip)], values_ref.at[pl.ds(q * strip, strip)])
+                for q in range(n_sum)
+            ),
         ),
         load_sem,
     )
@@ -461,7 +483,7 @@
             pltpu.SMEM(cone_scale.shape, jnp.float32),
             pltpu.VMEM(values.shape, jnp.bfloat16),
             pltpu.VMEM((cones, width), jnp.float32),
-            pltpu.SemaphoreType.DMA((4,)),
+            pltpu.SemaphoreType.DMA((3 + n_sum,)),
             pltpu.VMEM((cones, width), jnp.float32),
             pltpu.VMEM((n_tile, n_sum, SLOTS, strip, width), jnp.bfloat16),
             pltpu.VMEM((n_tile, 8, width), jnp.int32),
@@ -476,6 +498,7 @@
                 pltpu.SemaphoreType.DMA((n_tile, n_sum + 1)),
                 pltpu.SemaphoreType.DMA((13, n_sum)),
                 pltpu.SemaphoreType.DMA((n_tile, n_sum)),
+                pltpu.SemaphoreType.REGULAR,
             ]
         else:
             body = functools.partial(line_kernel, n_tile, n_cone, n_rep)

time: 19.9 us -> 19.5 us (0.980)
  Pallas kernels: 19.1 us -> 18.7 us
    pallas_call x1, Pallas kernels: 19.1 us -> 18.7 us  [per_device(): pl.pallas_call(body, out_shape=pltpu.VMEM((strip, n_tile * rows), jnp.flo...]
where the time goes in v7:
time: 19.5 us; the launch traced here: 19.3 us
  Pallas kernels  18.7 us (96%)
  local copies, waits for them, and re-layouts  0.63 us (3%)
    pallas_call x1, Pallas kernels, per_device(): pl.pallas_call(body, out_shape=pltpu.VMEM((strip, n_tile * rows), jnp.flo...  18.7 us
    unnamed x1, local copies, waits for them, and re-layouts  0.63 us

profile of v7, /device:TPU:0, one launch (start us, length us, event | category | flops | bytes accessed | tf_op | source)
XLA Modules:
  0.0 19.3 jit_solution(16326386670016110522)
XLA Ops:
  0.0 18.7 %shard_map.46 = f32[32,512]{1,0:T(8,128)S(1)} custom-call(s32[1,12]{1,0:T(1,128)} %pattern_hbm.1, f32[12]{0:T(128)} %scale_hbm.1, bf16[128,1536]{1,0:T(8,128)(2,1)} %values_hbm.1, f32[12,128]{1,0:T(8,128)} %point_hbm.1), custom_call_target="tpu_custom_call" | custom-call | tf_op jit(solution)/shard_map/pallas_call | solution.py:513
  18.7 0.6 %copy.6 = f32[32,512]{1,0:T(8,128)} copy(f32[32,512]{1,0:T(8,128)S(1)} %shard_map.46) | data formatting | bytes 131072

commit v8 on v7

--- a/solution.py
+++ b/solution.py
@@ -237,15 +237,16 @@
 
         arrive(far, n_sum)
         left = moved((me, near, twin), far)
-        for q in range(n_sum):
-            arrive(far, q)
-        right = wide(held.at[far])
-        block = outer(right, left)
-        put(9 + me - low, block[:, :width])
-        put(9 + near - low, block[:, width : 2 * width])
-        put(9 + twin - low, block[:, 2 * width :])
-        send(*far_send)
-        block = outer(left, right)
+        half = n_sum // 2
+        for first in (0, half):
+            for q in range(first, first + half):
+                arrive(far, q)
+            block = outer(wide(held.at[far, pl.ds(first, half)]), left).astype(PARTIAL)
+            for i, x in enumerate((me, near, twin)):
+                part[9 + x - low, pl.ds(first, half)] = block[:, i * width : (i + 1) * width].reshape(half, strip, width)
+            for q in range(first, first + half):
+                strip_copy(9, far, low, q, 3).start()
+        block = outer(left, wide(held.at[far]))
         put(8, block[:rows], far)
         put(6, block[rows : 2 * rows])
         put(12, block[2 * rows :])

time: 19.5 us -> 18.1 us (0.928)
  Pallas kernels: 18.7 us -> 17.3 us
    pallas_call x1, Pallas kernels: 18.7 us -> 17.3 us  [per_device(): pl.pallas_call(body, out_shape=pltpu.VMEM((strip, n_tile * rows), jnp.flo...]
where the time goes in v8:
time: 18.1 us; the launch traced here: 17.9 us
  Pallas kernels  17.3 us (96%)
  local copies, waits for them, and re-layouts  0.63 us (3%)
    pallas_call x1, Pallas kernels, per_device(): pl.pallas_call(body, out_shape=pltpu.VMEM((strip, n_tile * rows), jnp.flo...  17.3 us
    unnamed x1, local copies, waits for them, and re-layouts  0.63 us

profile of v8, /device:TPU:0, one launch (start us, length us, event | category | flops | bytes accessed | tf_op | source)
XLA Modules:
  0.0 17.9 jit_solution(9677783180461349413)
XLA Ops:
  0.0 17.3 %shard_map.46 = f32[32,512]{1,0:T(8,128)S(1)} custom-call(s32[1,12]{1,0:T(1,128)} %pattern_hbm.1, f32[12]{0:T(128)} %scale_hbm.1, bf16[128,1536]{1,0:T(8,128)(2,1)} %values_hbm.1, f32[12,128]{1,0:T(8,128)} %point_hbm.1), custom_call_target="tpu_custom_call" | custom-call | tf_op jit(solution)/shard_map/pallas_call | solution.py:514
  17.3 0.6 %copy.6 = f32[32,512]{1,0:T(8,128)} copy(f32[32,512]{1,0:T(8,128)S(1)} %shard_map.46) | data formatting | bytes 131072
